TPU v7x, 32 devices: a whole 2x2x4 slice. The times are simulated.
32 devices in a mesh: row: 8 (over z, core), col: 4 (over y, x).
Axes of the slice: x: 2, y: 2, z: 4, core: 2. Of those that a mesh axis runs over, the one named last changes fastest.
Arguments:
- blocks: bfloat16 [32, 48, 128, 128], P('row', 'col'), may hold values from -0.078125 to 0.078125
- columns: int32 [32, 48], P('row', 'col'), may hold values from 0 to 7
- counts: int32 [32, 4], P('row', 'col'), may hold values from 6 to 12, as said below
- inverse_diag: float32 [32, 128, 128], P('row')
- log_inverse_permeability: float32 [32, 128], P('row'), may hold values from -1 to 1
- base_velocity: float32 [32, 128], P('row'), may hold values from -6 to 6
- direction: float32 [32, 32, 128], P(None, 'row'), may hold values from -6 to 6
- obs_rows: int32 [1024], P('row'), may hold values from 0 to 3
- obs_weight: float32 [1024, 128], P('row'), may hold values from -0.5 to 0.5
- noise_prec: float32 [1024], P('row'), may hold values from 0.5 to 2
Outputs:
- hessian: float32 [32, 32, 128], P(None, 'row')
- predicted: float32 [32, 1024], P(None, 'row')
Inputs may be any that keep to these rules, and one draw needn't show every extreme that they name: `counts`: every index of row has a block row with all 12 slots live in each column group.
All inputs are finite; a program needn't handle non-finite values.
Results may differ from a plain program's by a relative error of at most 0.025.
Values may be sent and summed in bfloat16 or wider, within the bound.
A program may use at most 64 MiB of HBM per device.

v0:
```python
import jax
import jax.numpy as jnp
from jax import lax
from jax.sharding import PartitionSpec as P


def broadcast(value, axis, source):
    kept = jnp.where(lax.axis_index(axis) == source, value, 0).astype(value.dtype)
    return lax.psum(kept, axis)


def diag_apply(inverse_diag, values):
    return jnp.einsum("iab,sib->sia", inverse_diag, values, precision=lax.Precision.HIGHEST)


def diag_apply_t(inverse_diag, values):
    return jnp.einsum("iba,sib->sia", inverse_diag, values, precision=lax.Precision.HIGHEST)


def per_device(
    blocks,
    columns,
    counts,
    inverse_diag,
    log_inverse_permeability,
    base_velocity,
    direction,
    obs_rows,
    obs_weight,
    noise_prec,
):
    group_ratio = lax.axis_size("row") // lax.axis_size("col")
    row_index = lax.axis_index("row")
    col_index = lax.axis_index("col")
    nrows = blocks.shape[0]
    slot_count = blocks.shape[1]
    directions = direction.shape[0]
    trace_width = blocks.shape[2]
    group_width = nrows * group_ratio
    alpha_u = jnp.exp(log_inverse_permeability) * base_velocity
    forcing = -alpha_u[None] * direction
    live = jnp.arange(slot_count)[None, :] < counts
    flat_cols = columns.reshape(-1)
    trace_state = diag_apply(inverse_diag, forcing)
    for sweep in range(2):
        state_low = trace_state.astype(jnp.bfloat16)
        pieces = [
            broadcast(state_low, "row", col_index * group_ratio + member)
            for member in range(group_ratio)
        ]
        column_state = jnp.concatenate(pieces, axis=1)
        picked = jnp.take(column_state, flat_cols, axis=1).reshape(
            directions, nrows, slot_count, trace_width
        )
        picked = jnp.where(live[None, :, :, None], picked, jnp.zeros((), jnp.bfloat16))
        terms = jnp.einsum("ikab,sikb->sia", blocks, picked, preferred_element_type=jnp.float32)
        trace_state = diag_apply(inverse_diag, forcing - lax.psum(terms, "col"))
    onehot = (obs_rows[:, None] == jnp.arange(nrows)[None, :]).astype(jnp.float32)
    sampled_draws = jnp.einsum(
        "pa,sia->spi", obs_weight, trace_state, precision=lax.Precision.HIGHEST
    )
    predicted = jnp.sum(sampled_draws * onehot[None], axis=2)
    coupling = onehot[:, :, None] * obs_weight[:, None, :]
    adjoint_force = -jnp.einsum(
        "sp,pia->sia", predicted * noise_prec[None], coupling, precision=lax.Precision.HIGHEST
    )
    targets = jax.nn.one_hot(flat_cols, group_width, dtype=jnp.float32) * live.reshape(-1)[
        :, None
    ].astype(jnp.float32)
    adjoint = diag_apply_t(inverse_diag, adjoint_force)
    for sweep in range(2):
        contrib = jnp.einsum(
            "ikab,sia->sikb",
            blocks,
            adjoint.astype(jnp.bfloat16),
            preferred_element_type=jnp.float32,
        )
        contrib = contrib.reshape(directions, nrows * slot_count, trace_width)
        column_part = jnp.einsum("snb,nj->sjb", contrib, targets, precision=lax.Precision.HIGHEST)
        column_share = lax.psum_scatter(
            column_part.astype(jnp.bfloat16), "row", scatter_dimension=0, tiled=True
        ).astype(jnp.float32)
        outgoing = jnp.tile(column_share, (1, lax.axis_size("col"), 1))
        owned = lax.all_to_all(
            outgoing.astype(jnp.bfloat16), "row", split_axis=1, concat_axis=0, tiled=True
        ).astype(outgoing.dtype)
        returned = broadcast(owned.astype(jnp.bfloat16), "col", row_index // group_ratio).astype(
            owned.dtype
        )
        adjoint = diag_apply_t(inverse_diag, adjoint_force - returned)
    hessian = -alpha_u[None] * adjoint
    return (hessian, predicted)


def solution(mesh):
    placed = (
        P("row", "col", None, None),
        P("row", "col"),
        P("row", "col"),
        P("row", None, None),
        P("row", None),
        P("row", None),
        P(None, "row", None),
        P("row"),
        P("row", None),
        P("row"),
    )
    return jax.shard_map(
        per_device,
        mesh=mesh,
        in_specs=placed,
        out_specs=(P(None, "row", None), P(None, "row")),
        check_vma=False,
    )
```

profile of v0, /device:TPU:0, one launch (start us, length us, event | category | flops | bytes accessed | tf_op | source)
XLA Modules:
  0.0 335.7 jit_solution(4297615082807681327)
XLA Ops:
  7.2 0.8 multiply_negate_fusion
  8.1 0.9 broadcast_multiply_fusion
  8.9 2.1 select_bitcast_fusion.3
  11.1 0.8 reshape.131
  11.9 0.7 fusion.46
  12.6 55.1 %all-reduce.13.cloned.1.call-done = (bf16[32,4,128]{2,0,1:T(8,128)(2,1)}, bf16[32,4,128]{2,0,1:T(8,128)(2,1)}) async-done(((bf16[32,4,128]{2,0,1:T(8,128)(2,1)}, bf16[32,4,128]{2,0,1:T(8,128)(2,1)}), (bf16[32,4,128]{2,0,1:T(8,128)(2,1)}, bf16[32,4,128]{2,0,1:T(8,128)(2,1)})) %all-reduce.13.cloned.1.call-update) | async-done | bytes 65552 | tf_op jit(solution)/shard_map/psum | solution.py:9
  67.6 0.8 pad_maximum_fusion
  70.6 41.2 %all-reduce.7.cloned.1.call-done = f32[32,4,128]{2,1,0:T(4,128)} async-done(((f32[32,4,128]{2,1,0:T(4,128)}), f32[32,4,128]{2,1,0:T(4,128)}) %all-reduce.7.cloned.1.call-update) | async-done | bytes 65552 | tf_op jit(solution)/shard_map/psum | solution.py:57
  111.9 0.9 fusion.68
  112.7 1.1 select_bitcast_fusion.1
  113.9 54.6 %all-reduce.11.cloned.1.call-done = (bf16[32,4,128]{2,0,1:T(8,128)(2,1)}, bf16[32,4,128]{2,0,1:T(8,128)(2,1)}) async-done(((bf16[32,4,128]{2,0,1:T(8,128)(2,1)}, bf16[32,4,128]{2,0,1:T(8,128)(2,1)}), (bf16[32,4,128]{2,0,1:T(8,128)(2,1)}, bf16[32,4,128]{2,0,1:T(8,128)(2,1)})) %all-reduce.11.cloned.1.call-update) | async-done | bytes 65552 | tf_op jit(solution)/shard_map/psum | solution.py:9
  168.5 0.8 pad_maximum_fusion.1
  171.6 41.0 %all-reduce.9.cloned.1.call-done = f32[32,4,128]{2,1,0:T(4,128)} async-done(((f32[32,4,128]{2,1,0:T(4,128)}), f32[32,4,128]{2,1,0:T(4,128)}) %all-reduce.9.cloned.1.call-update) | async-done | bytes 65552 | tf_op jit(solution)/shard_map/psum | solution.py:57
  212.6 0.9 fusion.67
  215.3 1.5 fusion
  216.9 30.3 %reduce-scatter.3.cloned.1.call-done = bf16[4,8,128]{2,1,0:T(8,128)(2,1)} async-done(((bf16[32,8,128]{2,1,0:T(8,128)(2,1)}), bf16[4,8,128]{2,1,0:T(8,128)(2,1)}) %reduce-scatter.3.cloned.1.call-update) | async-done | bytes 8208 | tf_op jit(solution)/shard_map/reduce_scatter | solution.py:80
  247.1 0.7 copy.22
  248.5 3.3 all-to-all-start
  251.9 5.6 %all-to-all-done = bf16[4,32,128]{2,0,1:T(4,128)(2,1)S(1)} async-done(((bf16[4,32,128]{2,0,1:T(4,128)(2,1)}), bf16[4,32,128]{2,0,1:T(4,128)(2,1)S(1)}, u32[]{:S(2)}, u32[]{:S(2)}) %all-to-all-start) | async-done | bytes 32800 | tf_op jit(solution)/shard_map/all_to_all | solution.py:84
  257.5 16.3 %psum.62 = bf16[32,4,128]{2,0,1:T(8,128)(2,1)S(1)} all-reduce(bf16[32,4,128]{2,0,1:T(8,128)(2,1)S(1)} %bitcast.118), channel_id=1, replica_groups=mesh['row'=8,'col'=4] {'col'}, use_global_device_ids=true, to_apply=%region_8.10 | all-reduce | flops 16384 | bytes 65536 | tf_op jit(solution)/shard_map/psum | solution.py:9
  274.5 1.5 fusion.1
  276.1 26.6 %reduce-scatter.5.cloned.1.call-done = bf16[4,8,128]{2,1,0:T(8,128)(2,1)} async-done(((bf16[32,8,128]{2,1,0:T(8,128)(2,1)}), bf16[4,8,128]{2,1,0:T(8,128)(2,1)}) %reduce-scatter.5.cloned.1.call-update) | async-done | bytes 8208 | tf_op jit(solution)/shard_map/reduce_scatter | solution.py:80
  303.4 8.1 %all_to_all.8 = bf16[4,32,128]{2,0,1:T(4,128)(2,1)S(1)} all-to-all(bf16[4,32,128]{2,0,1:T(4,128)(2,1)S(1)} %bitcast.115), channel_id=1, replica_groups=mesh['row'=8,'col'=4] {'row'}, dimensions={1} | all-to-all | bytes 65536 | tf_op jit(solution)/shard_map/all_to_all | solution.py:84
  311.5 16.3 %psum.63 = bf16[32,4,128]{2,0,1:T(8,128)(2,1)S(1)} all-reduce(bf16[32,4,128]{2,0,1:T(8,128)(2,1)S(1)} %bitcast.119), channel_id=1, replica_groups=mesh['row'=8,'col'=4] {'col'}, use_global_device_ids=true, to_apply=%region_10.12 | all-reduce | flops 16384 | bytes 65536 | tf_op jit(solution)/shard_map/psum | solution.py:9
  (58 shorter events, 9.6 us)
Async XLA Ops:
  7.2 62.1 %copy-start = (bf16[4,12,128,128]{3,2,1,0:T(8,128)(2,1)S(1)}, bf16[4,12,128,128]{3,2,1,0:T(8,128)(2,1)}, u32[]{:S(2)}) copy-start(bf16[4,12,128,128]{3,2,1,0:T(8,128)(2,1)} %param.12) | copy-start | bytes 4718596
  7.2 60.5 %all-reduce.13.cloned.1.call-start = ((), (), s32[]{:S(2)}) async-start(), calls=%async_computation.9 | async-start | bytes 131072 | tf_op jit(solution)/shard_map/psum | solution.py:9
  11.0 100.8 %all-reduce.7.cloned.1.call-start = ((), (), s32[]{:S(2)}) async-start(), calls=%async_computation.4 | async-start | bytes 131072 | tf_op jit(solution)/shard_map/psum | solution.py:57
  69.1 42.8 %copy-start.2 = (f32[32,4,128]{2,1,0:T(4,128)S(1)}, f32[32,4,128]{2,1,0:T(4,128)}, u32[]{:S(2)}) copy-start(f32[32,4,128]{2,1,0:T(4,128)} %param.18) | copy-start | bytes 196612
  69.1 43.6 %copy-start.1 = (f32[4,128,128]{2,1,0:T(8,128)S(1)}, f32[4,128,128]{2,1,0:T(8,128)}, u32[]{:S(2)}) copy-start(f32[4,128,128]{2,1,0:T(8,128)} %param.15) | copy-start | bytes 786436
  70.6 97.9 %all-reduce.11.cloned.1.call-start = ((), (), s32[]{:S(2)}) async-start(), calls=%async_computation.8 | async-start | bytes 131072 | tf_op jit(solution)/shard_map/psum | solution.py:9
  113.9 98.7 %all-reduce.9.cloned.1.call-start = ((), (), s32[]{:S(2)}) async-start(), calls=%async_computation.5 | async-start | bytes 131072 | tf_op jit(solution)/shard_map/psum | solution.py:57
  169.9 1.6 copy-start.6
  170.1 43.9 %copy-start.3 = (f32[128,128]{1,0:T(8,128)S(1)}, f32[128,128]{1,0:T(8,128)}, u32[]{:S(2)}) copy-start(f32[128,128]{1,0:T(8,128)} %param.20) | copy-start | bytes 196612
  170.1 44.1 %copy-start.5 = (f32[128]{0:T(128)S(1)}, f32[128]{0:T(128)}, u32[]{:S(2)}) copy-start(f32[128]{0:T(128)} %param.21) | copy-start | bytes 1540
  171.5 75.7 %reduce-scatter.3.cloned.1.call-start = ((), (), s32[]{:S(2)}) async-start(), calls=%async_computation.6 | async-start | bytes 73728 | tf_op jit(solution)/shard_map/reduce_scatter | solution.py:80
  214.2 2.6 copy-start.4
  248.5 9.0 %all-to-all-start = ((bf16[4,32,128]{2,0,1:T(4,128)(2,1)}), bf16[4,32,128]{2,0,1:T(4,128)(2,1)S(1)}, u32[]{:S(2)}, u32[]{:S(2)}) async-start(bf16[4,32,128]{2,0,1:T(4,128)(2,1)} %bitcast.24), calls=%async_computation.1 | async-start | bytes 65536 | tf_op jit(solution)/shard_map/all_to_all | solution.py:84
  251.8 50.9 %reduce-scatter.5.cloned.1.call-start = ((), (), s32[]{:S(2)}) async-start(), calls=%async_computation.7 | async-start | bytes 73728 | tf_op jit(solution)/shard_map/reduce_scatter | solution.py:80
Sparse Core Ops, SparseCore 0:
  11.1 56.4 all-reduce.12
  71.3 40.4 all-reduce.6
  114.8 53.6 all-reduce.10
  172.1 40.4 all-reduce.8
  217.0 30.0 reduce-scatter.2
  276.2 26.3 reduce-scatter.4
where the time goes:
time: 336 us
  waiting for transfers between devices  254 us (76%)
  blocking collectives  40.7 us (12%)
  between operations  14.3 us (4%)
  matrix products  10.5 us (3%)
  local copies, waits for them, and re-layouts  6.29 us (2%)
  other arithmetic  5.94 us (2%)
  starting transfers between devices  3.59 us (1%)
    psum x2, waiting for transfers between devices, broadcast(): return lax.psum(kept, axis)  110 us
    psum x2, waiting for transfers between devices, per_device(): trace_state = diag_apply(inverse_diag, forcing - lax.psum(terms, 'col'))  82.2 us
    reduce_scatter x2, waiting for transfers between devices, per_device(): lax.psum_scatter(column_part.astype(jnp.bfloat16), 'row', scatter_dimensi...  56.8 us
    psum x2, blocking collectives, broadcast(): return lax.psum(kept, axis)  32.6 us
    all_to_all x1, blocking collectives, per_device(): lax.all_to_all(outgoing.astype(jnp.bfloat16), 'row', split_axis=1, concat...  8.12 us
  transfers between devices with their start and end apart: 7, of which 7 were waited for; matrix products, arithmetic and copies ran while one was open for 0% of the time, Pallas kernels for 0%

commit v1 on v0

v1 whole, which is shorter than its diff:
```python
import functools

import jax
import jax.numpy as jnp
from jax import lax
from jax.experimental import pallas as pl
from jax.experimental.pallas import tpu as pltpu
from jax.sharding import PartitionSpec as P

F32 = jnp.float32
BF16 = jnp.bfloat16
SWEEPS = 2


def flip(index, bits, size):
    total, bit = 0, 1
    while bit < size:
        digit = lax.rem(lax.div(index, jnp.int32(bit)), jnp.int32(2))
        total = total + bit * (1 - digit if (bits // bit) % 2 else digit)
        bit *= 2
    return total


def split(values):
    high = values.astype(BF16)
    return high, (values - high.astype(F32)).astype(BF16)


def matmul(left, right):
    return lax.dot_general(left, right, (((1,), (0,)), ((), ())), preferred_element_type=F32)


def matmul_t(left, right):
    return lax.dot_general(left, right, (((1,), (1,)), ((), ())), preferred_element_type=F32)


def wide_matmul(values, pair):
    rows, width = values.shape[0], pair.shape[1] // 2
    high = values.astype(BF16).astype(F32)
    both = jnp.concatenate([high, values - high], axis=0).astype(BF16)
    out = matmul(both, pair)
    return out[:rows, :width] + out[:rows, width:] + out[rows:, :width]


def kernel(
    ncol,
    nmem,
    columns_ref,
    counts_ref,
    blocks_hbm,
    diag_ref,
    logperm_ref,
    velocity_ref,
    direction_ref,
    obs_rows_ref,
    obs_weight_ref,
    prec_ref,
    hess_ref,
    pred_ref,
    blk,
    merged,
    diag_f,
    diag_a,
    obs_f,
    obs_a,
    part,
    zf,
    xf,
    rs_out,
    rs_in,
    yb,
    ad_out,
    ad_in,
    za_out,
    za,
    hb,
    pb,
    blk_sem,
    zf_s,
    zf_r,
    xf_s,
    xf_r,
    rs_s,
    rs_r,
    yb_s,
    yb_r,
    ad_s,
    ad_r,
    za_s,
    za_r,
    hb_s,
    hb_r,
    pb_s,
    pb_r,
):
    row = lax.axis_index("row")
    col = lax.axis_index("col")
    quad = lax.div(row, jnp.int32(nmem))
    mem = lax.rem(row, jnp.int32(nmem))
    nrows, nslots, width = blk.shape[0], blk.shape[1], blk.shape[2]
    share = direction_ref.shape[0] // ncol
    nblk = nmem * nrows

    def device(q, k, c):
        return (q * nmem + k, c)

    def copy(src, dst, send, recv, target):
        return pltpu.make_async_remote_copy(
            src_ref=src,
            dst_ref=dst,
            send_sem=send,
            recv_sem=recv,
            device_id=target,
            device_id_type=pl.DeviceIdType.MESH,
        )

    def landed(slot, recv):
        copy(slot, slot, recv, recv, (row, col)).wait_recv()

    def block_row(piece, i):
        return piece[i * share : (i + 1) * share]

    def stack(pieces):
        return jnp.concatenate(pieces, axis=0)

    def diag_apply(pairs, piece):
        return stack([wide_matmul(block_row(piece, i), pairs[i]) for i in range(nrows)])

    barrier = pltpu.get_barrier_semaphore()
    peers = [(flip(quad, f, ncol), mem, col) for f in range(1, ncol)]
    peers += [
        (quad, flip(mem, x, nmem), flip(col, e, ncol))
        for e in range(ncol)
        for x in range(nmem)
        if e or x
    ]
    for q, k, c in peers:
        pl.semaphore_signal(
            barrier, inc=1, device_id=device(q, k, c), device_id_type=pl.DeviceIdType.MESH
        )
    fetches = [
        pltpu.make_async_copy(blocks_hbm.at[i], blk.at[i], blk_sem.at[i]) for i in range(nrows)
    ]
    for fetch in fetches:
        fetch.start()

    alpha = jnp.exp(logperm_ref[...]) * velocity_ref[...]
    for i in range(nrows):
        high, low = split(diag_ref[i].T)
        diag_f[i, :, :width] = high
        diag_f[i, :, width:] = low
    mine = direction_ref[pl.ds(col * share, share)]
    forcing = stack([-alpha[i : i + 1] * mine[:, i, :] for i in range(nrows)])
    base = diag_apply(diag_f, forcing)

    def merge(i):
        fetches[i].wait()
        count = counts_ref[i, 0]
        target = [
            jnp.where(jnp.int32(k) < count, columns_ref[i, k], jnp.int32(-1))
            for k in range(nslots)
        ]

        def body(pair, carry):
            for half in range(2):
                j = pair * 2 + half
                total = jnp.zeros((width, width), F32)
                for k in range(nslots):
                    keep = jnp.where(target[k] == j, jnp.float32(1), jnp.float32(0))
                    total = total + keep * blk[i, k].astype(F32)
                at = pl.ds(pl.multiple_of(j * width, width), width)
                merged[i * width : (i + 1) * width, at] = total.astype(BF16)
            return carry

        lax.fori_loop(0, nblk // 2, body, 0)

    sent = []

    def start(item, when=None):
        if when is None:
            item.start()
        else:
            pl.when(when)(item.start)
        sent.append((item, when))

    def spread_along_row(t, piece):
        zf[t, quad] = piece.astype(BF16)
        for f in range(1, ncol):
            q = flip(quad, f, ncol)
            start(
                copy(
                    zf.at[t, quad],
                    zf.at[t, quad],
                    zf_s.at[t, f],
                    zf_r.at[t, quad],
                    device(q, mem, col),
                )
            )

    def forward_to_column(t):
        for f in range(ncol):
            q = flip(quad, f, ncol)
            if f:
                landed(zf.at[t, q], zf_r.at[t, q])
            for x in range(nmem):
                start(
                    copy(
                        zf.at[t, q],
                        xf.at[t, mem, col],
                        xf_s.at[t, f, x],
                        xf_r.at[t, mem, col],
                        device(quad, flip(mem, x, nmem), q),
                    ),
                    None if x else q != col,
                )
        xf[t, mem, col] = zf[t, col]

    def column_state(t):
        for e in range(ncol):
            for x in range(nmem):
                if e or x:
                    k, c = flip(mem, x, nmem), flip(col, e, ncol)
                    landed(xf.at[t, k, c], xf_r.at[t, k, c])
        lanes = []
        for k in range(nmem):
            pieces = [xf[t, k, c].astype(F32) for c in range(ncol)]
            for i in range(nrows):
                lanes.append(stack([block_row(piece, i) for piece in pieces]))
        return jnp.concatenate(lanes, axis=1).astype(BF16)

    def sum_over_columns(t, terms):
        for c in range(ncol):
            rows = terms[c * share : (c + 1) * share]
            piece = stack([rows[:, i * width : (i + 1) * width] for i in range(nrows)])
            part[t, c] = piece
            rs_out[t, c] = piece.astype(BF16)
        for e in range(1, ncol):
            c = flip(col, e, ncol)
            start(
                copy(
                    rs_out.at[t, c],
                    rs_in.at[t, col],
                    rs_s.at[t, e],
                    rs_r.at[t, col],
                    device(quad, mem, c),
                )
            )
        total = part[t, col]
        for e in range(1, ncol):
            c = flip(col, e, ncol)
            landed(rs_in.at[t, c], rs_r.at[t, c])
            total = total + rs_in[t, c].astype(F32)
        return total

    def gather_start(buf, at, send, recv):
        for e in range(1, ncol):
            start(
                copy(
                    buf.at[at + (col,)],
                    buf.at[at + (col,)],
                    send.at[at + (e,)],
                    recv.at[at + (col,)],
                    device(quad, mem, flip(col, e, ncol)),
                )
            )

    def gather_wait(buf, at, recv):
        for e in range(1, ncol):
            c = flip(col, e, ncol)
            landed(buf.at[at + (c,)], recv.at[at + (c,)])

    state = base
    for t in range(SWEEPS):
        if t == 0:
            pl.semaphore_wait(barrier, len(peers))
        spread_along_row(t, state)
        if t == 0:
            for i in range(nrows // 2):
                merge(i)
        forward_to_column(t)
        if t == 0:
            for i in range(nrows // 2, nrows):
                merge(i)
        terms = matmul_t(column_state(t), merged[...])
        if t == 0:
            for i in range(nrows):
                high, low = split(diag_ref[i])
                diag_a[i, :, :width] = high
                diag_a[i, :, width:] = low
            high, low = split(obs_weight_ref[...])
            points = obs_weight_ref.shape[0]
            obs_a[:, :width] = high
            obs_a[:, width:] = low
            high, low = split(obs_weight_ref[...].T)
            obs_f[:, :points] = high
            obs_f[:, points:] = low
        state = base - diag_apply(diag_f, sum_over_columns(t, terms))

    sampled = wide_matmul(state, obs_f[...])
    chosen = [(obs_rows_ref[...] == i).astype(F32) for i in range(nrows)]
    predicted = sum(block_row(sampled, i) * chosen[i] for i in range(nrows))
    weighted = predicted * prec_ref[...]
    force = -wide_matmul(stack([weighted * chosen[i] for i in range(nrows)]), obs_a[...])
    adjoint = diag_apply(diag_a, force)

    for t in range(SWEEPS):
        yb[t, col] = adjoint.astype(BF16)
        gather_start(yb, (t,), yb_s, yb_r)
        if t == 0:
            pb[col] = predicted
            gather_start(pb, (), pb_s, pb_r)
        gather_wait(yb, (t,), yb_r)
        pieces = [yb[t, c].astype(F32) for c in range(ncol)]
        lanes = [stack([block_row(piece, i) for piece in pieces]) for i in range(nrows)]
        terms = matmul(jnp.concatenate(lanes, axis=1).astype(BF16), merged[...])
        for k in range(nmem):
            for c in range(ncol):
                rows = terms[c * share : (c + 1) * share]
                ad_out[t, k, c] = stack(
                    [
                        rows[:, (k * nrows + i) * width : (k * nrows + i + 1) * width]
                        for i in range(nrows)
                    ]
                ).astype(BF16)
        for e in range(ncol):
            for x in range(nmem):
                if e or x:
                    k, c = flip(mem, x, nmem), flip(col, e, ncol)
                    start(
                        copy(
                            ad_out.at[t, k, c],
                            ad_in.at[t, mem, col],
                            ad_s.at[t, x, e],
                            ad_r.at[t, mem, col],
                            device(quad, k, c),
                        )
                    )
        ad_in[t, mem, col] = ad_out[t, mem, col]
        for e in range(ncol):
            c = flip(col, e, ncol)
            for x in range(nmem):
                if e or x:
                    k = flip(mem, x, nmem)
                    landed(ad_in.at[t, k, c], ad_r.at[t, k, c])
            total = sum(ad_in[t, k, c].astype(F32) for k in range(nmem))
            za_out[t, c] = total.astype(BF16)
            start(
                copy(
                    za_out.at[t, c],
                    za.at[t, quad],
                    za_s.at[t, e],
                    za_r.at[t, quad],
                    device(c, mem, col),
                ),
                c != quad,
            )
        total = za_out[t, quad].astype(F32)
        for f in range(1, ncol):
            q = flip(quad, f, ncol)
            landed(za.at[t, q], za_r.at[t, q])
            total = total + za[t, q].astype(F32)
        adjoint = diag_apply(diag_a, force - total)

    hb[col] = stack(
        [-alpha[i : i + 1] * block_row(adjoint, i) for i in range(nrows)]
    ).astype(BF16)
    gather_start(hb, (), hb_s, hb_r)
    gather_wait(pb, (), pb_r)
    for c in range(ncol):
        pred_ref[c * share : (c + 1) * share, :] = pb[c]
    gather_wait(hb, (), hb_r)
    for c in range(ncol):
        piece = hb[c].astype(F32)
        for i in range(nrows):
            hess_ref[c * share : (c + 1) * share, i, :] = block_row(piece, i)

    for item, when in sent:
        if when is None:
            item.wait_send()
        else:
            pl.when(when)(item.wait_send)


def per_device(
    blocks,
    columns,
    counts,
    inverse_diag,
    log_inverse_permeability,
    base_velocity,
    direction,
    obs_rows,
    obs_weight,
    noise_prec,
):
    ncol = lax.axis_size("col")
    nmem = lax.axis_size("row") // ncol
    nrows, nslots, width, _ = blocks.shape
    directions, points = direction.shape[0], obs_weight.shape[0]
    share = directions // ncol
    rows = nrows * share
    dma = pltpu.SemaphoreType.DMA
    vmem = pl.BlockSpec(memory_space=pltpu.VMEM)
    smem = pl.BlockSpec(memory_space=pltpu.SMEM)

    def pieces(*lead):
        return pltpu.VMEM(lead + (rows, width), BF16)

    s, c, g = SWEEPS, ncol, nmem
    return pl.pallas_call(
        functools.partial(kernel, ncol, nmem),
        out_shape=(
            jax.ShapeDtypeStruct(direction.shape, F32),
            jax.ShapeDtypeStruct((directions, points), F32),
        ),
        in_specs=[smem, smem, pl.BlockSpec(memory_space=pl.ANY)] + [vmem] * 7,
        out_specs=(vmem, vmem),
        scratch_shapes=[
            pltpu.VMEM(blocks.shape, BF16),
            pltpu.VMEM((nrows * width, nmem * nrows * width), BF16),
            pltpu.VMEM((nrows, width, 2 * width), BF16),
            pltpu.VMEM((nrows, width, 2 * width), BF16),
            pltpu.VMEM((width, 2 * points), BF16),
            pltpu.VMEM((points, 2 * width), BF16),
            pltpu.VMEM((s, c, rows, width), F32),
            pieces(s, c),
            pieces(s, g, c),
            pieces(s, c),
            pieces(s, c),
            pieces(s, c),
            pieces(s, g, c),
            pieces(s, g, c),
            pieces(s, c),
            pieces(s, c),
            pieces(c),
            pltpu.VMEM((c, share, points), F32),
            dma((nrows,)),
            dma((s, c)),
            dma((s, c)),
            dma((s, c, g)),
            dma((s, g, c)),
            dma((s, c)),
            dma((s, c)),
            dma((s, c)),
            dma((s, c)),
            dma((s, g, c)),
            dma((s, g, c)),
            dma((s, c)),
            dma((s, c)),
            dma((c,)),
            dma((c,)),
            dma((c,)),
            dma((c,)),
        ],
        compiler_params=pltpu.CompilerParams(
            collective_id=0, has_side_effects=True, vmem_limit_bytes=32 * 1024 * 1024
        ),
    )(
        columns,
        counts,
        blocks,
        inverse_diag,
        log_inverse_permeability,
        base_velocity,
        direction,
        obs_rows.reshape(1, points),
        obs_weight,
        noise_prec.reshape(1, points),
    )


def solution(mesh):
    placed = (
        P("row", "col", None, None),
        P("row", "col"),
        P("row", "col"),
        P("row", None, None),
        P("row", None),
        P("row", None),
        P(None, "row", None),
        P("row"),
        P("row", None),
        P("row"),
    )
    return jax.shard_map(
        per_device,
        mesh=mesh,
        in_specs=placed,
        out_specs=(P(None, "row", None), P(None, "row")),
        check_vma=False,
    )
```

time: 336 us -> 62.3 us (0.19)
  waiting for transfers between devices: 254 us -> 0 us
  Pallas kernels: 0 us -> 51.9 us
  blocking collectives: 40.7 us -> 0 us
  between operations: 14.3 us -> 0.65 us
  matrix products: 10.5 us -> 0 us
  other arithmetic: 5.94 us -> 0 us
  starting transfers between devices: 3.59 us -> 0 us
    psum x4 -> x0, waiting for transfers between devices: 192 us -> none  [the longest x2 110 us: broadcast(): return lax.psum(kept, axis)]
    reduce_scatter x2 -> x0, waiting for transfers between devices: 56.8 us -> none  [per_device(): lax.psum_scatter(column_part.astype(jnp.bfloat16), 'row', scatter_dimensi...]
    pallas_call x0 -> x1, Pallas kernels: none -> 51.9 us  [per_device(): pl.pallas_call(functools.partial(kernel, ncol, nmem), out_shape=(jax.Shap...]
    psum x2 -> x0, blocking collectives: 32.6 us -> none  [broadcast(): return lax.psum(kept, axis)]
    dot_general x14 -> x0, matrix products: 10.5 us -> none  [the longest x3 3.75 us: diag_apply(): jnp.einsum('iab,sib->sia', inverse_diag, values, precision=lax.Precision....]
    unnamed x18 -> x21, local copies, waits for them, and re-layouts: 0.73 us -> 9.37 us
    all_to_all x1 -> x0, blocking collectives: 8.12 us -> none  [per_device(): lax.all_to_all(outgoing.astype(jnp.bfloat16), 'row', split_axis=1, concat...]
    all_to_all x1 -> x0, waiting for transfers between devices: 5.61 us -> none  [per_device(): lax.all_to_all(outgoing.astype(jnp.bfloat16), 'row', split_axis=1, concat...]
  transfers between devices with their start and end apart: 7 -> 0, of which waited for: 7 -> 0; matrix products, arithmetic and copies ran while one was open for 0% -> 0% of each run, Pallas kernels for 0% -> 0%
where the time goes in v1:
time: 62.3 us; the launch traced here: 61.9 us
  Pallas kernels  51.9 us (83%)
  local copies, waits for them, and re-layouts  9.37 us (15%)
  between operations  0.65 us (1%)
    pallas_call x1, Pallas kernels, per_device(): pl.pallas_call(functools.partial(kernel, ncol, nmem), out_shape=(jax.Shap...  51.9 us
    unnamed x21, local copies, waits for them, and re-layouts  9.37 us

profile of v1, /device:TPU:0, one launch (start us, length us, event | category | flops | bytes accessed | tf_op | source)
XLA Modules:
  0.0 61.9 jit_solution(7281461084238360543)
XLA Ops:
  0.6 0.7 %copy.12.counts_ref = s32[4,1]{1,0:T(4,128)S(1)} copy(s32[4,1]{0,1:T(1,128)} %param.12) | data formatting | bytes 32 | tf_op args[2]
  1.4 0.0 copy-start
  1.4 1.4 %copy-done = bf16[4,12,128,128]{3,2,1,0:T(8,128)(2,1)S(1)} copy-done((bf16[4,12,128,128]{3,2,1,0:T(8,128)(2,1)S(1)}, bf16[4,12,128,128]{3,2,1,0:T(8,128)(2,1)}, u32[]{:S(2)}) %copy-start) | copy-done | bytes 1572888
  2.8 0.0 copy-start.1
  2.8 0.9 %copy-done.1 = f32[4,128,128]{2,1,0:T(8,128)S(1)} copy-done((f32[4,128,128]{2,1,0:T(8,128)S(1)}, f32[4,128,128]{2,1,0:T(8,128)}, u32[]{:S(2)}) %copy-start.1) | copy-done | bytes 262168
  3.7 0.0 copy-start.2
  3.7 0.8 %copy-done.2 = f32[32,4,128]{2,1,0:T(4,128)S(1)} copy-done((f32[32,4,128]{2,1,0:T(4,128)S(1)}, f32[32,4,128]{2,1,0:T(4,128)}, u32[]{:S(2)}) %copy-start.2) | copy-done | bytes 65560
  4.6 0.0 copy-start.3
  4.6 0.8 %copy-done.3 = f32[128,128]{1,0:T(8,128)S(1)} copy-done((f32[128,128]{1,0:T(8,128)S(1)}, f32[128,128]{1,0:T(8,128)}, u32[]{:S(2)}) %copy-start.3) | copy-done | bytes 65560
  5.4 0.0 copy-start.4
  5.4 0.7 %copy-done.4 = s32[4,12]{1,0:T(4,128)S(1)} copy-done((s32[4,12]{1,0:T(4,128)S(1)}, s32[4,12]{1,0:T(4,128)}, u32[]{:S(2)}) %copy-start.4) | copy-done | bytes 216
  6.1 0.0 copy-start.5
  6.1 0.7 %copy-done.5 = f32[4,128]{1,0:T(4,128)S(1)} copy-done((f32[4,128]{1,0:T(4,128)S(1)}, f32[4,128]{1,0:T(4,128)}, u32[]{:S(2)}) %copy-start.5) | copy-done | bytes 2072
  6.8 0.0 copy-start.6
  6.8 0.7 %copy-done.6 = f32[4,128]{1,0:T(4,128)S(1)} copy-done((f32[4,128]{1,0:T(4,128)S(1)}, f32[4,128]{1,0:T(4,128)}, u32[]{:S(2)}) %copy-start.6) | copy-done | bytes 2072
  7.5 0.0 copy-start.7
  7.5 0.7 %copy-done.7 = s32[128]{0:T(128)S(1)} copy-done((s32[128]{0:T(128)S(1)}, s32[128]{0:T(128)}, u32[]{:S(2)}) %copy-start.7) | copy-done | bytes 536
  8.1 0.0 copy-start.8
  8.1 0.7 %copy-done.8 = f32[128]{0:T(128)S(1)} copy-done((f32[128]{0:T(128)S(1)}, f32[128]{0:T(128)}, u32[]{:S(2)}) %copy-start.8) | copy-done | bytes 536
  8.8 51.9 %shard_map.113 = (f32[32,4,128]{2,1,0:T(4,128)S(1)}, f32[32,128]{1,0:T(8,128)S(1)}) custom-call(s32[4,12]{1,0:T(4,128)S(1)} %copy-done.4, s32[4,1]{1,0:T(4,128)S(1)} %copy.12.counts_ref, bf16[4,12,128,128]{3,2,1,0:T(8,128)(2,1)S(1)} %copy-done, f32[4,128,128]{2,1,0:T(8,128)S(1)} %copy-done.1, f32[4,128]{1,0:T(4,128)S(1)} %copy-done.5, ...), custom_call_target="tpu_custom_call" | custom-call | tf_op jit(solution)/shard_map/pallas_call | solution.py:410
  60.7 0.6 %copy.15 = f32[32,4,128]{2,1,0:T(4,128)} copy(f32[32,4,128]{2,1,0:T(4,128)S(1)} %get-tuple-element.4) | data formatting | bytes 131072
  61.3 0.6 copy.16
Async XLA Ops:
  1.4 1.4 %copy-start = (bf16[4,12,128,128]{3,2,1,0:T(8,128)(2,1)S(1)}, bf16[4,12,128,128]{3,2,1,0:T(8,128)(2,1)}, u32[]{:S(2)}) copy-start(bf16[4,12,128,128]{3,2,1,0:T(8,128)(2,1)} %blocks_hbm.1) | copy-start | bytes 4718596
  2.8 0.9 %copy-start.1 = (f32[4,128,128]{2,1,0:T(8,128)S(1)}, f32[4,128,128]{2,1,0:T(8,128)}, u32[]{:S(2)}) copy-start(f32[4,128,128]{2,1,0:T(8,128)} %diag_ref.1) | copy-start | bytes 786436
  3.7 0.8 %copy-start.2 = (f32[32,4,128]{2,1,0:T(4,128)S(1)}, f32[32,4,128]{2,1,0:T(4,128)}, u32[]{:S(2)}) copy-start(f32[32,4,128]{2,1,0:T(4,128)} %direction_ref.1) | copy-start | bytes 196612
  4.6 0.8 %copy-start.3 = (f32[128,128]{1,0:T(8,128)S(1)}, f32[128,128]{1,0:T(8,128)}, u32[]{:S(2)}) copy-start(f32[128,128]{1,0:T(8,128)} %obs_weight_ref.1) | copy-start | bytes 196612
  5.4 0.7 %copy-start.4 = (s32[4,12]{1,0:T(4,128)S(1)}, s32[4,12]{1,0:T(4,128)}, u32[]{:S(2)}) copy-start(s32[4,12]{1,0:T(4,128)} %columns_ref.1) | copy-start | bytes 580
  6.1 0.7 %copy-start.5 = (f32[4,128]{1,0:T(4,128)S(1)}, f32[4,128]{1,0:T(4,128)}, u32[]{:S(2)}) copy-start(f32[4,128]{1,0:T(4,128)} %logperm_ref.1) | copy-start | bytes 6148
  6.8 0.7 %copy-start.6 = (f32[4,128]{1,0:T(4,128)S(1)}, f32[4,128]{1,0:T(4,128)}, u32[]{:S(2)}) copy-start(f32[4,128]{1,0:T(4,128)} %velocity_ref.1) | copy-start | bytes 6148
  7.5 0.7 %copy-start.7 = (s32[128]{0:T(128)S(1)}, s32[128]{0:T(128)}, u32[]{:S(2)}) copy-start(s32[128]{0:T(128)} %param.17) | copy-start | bytes 1540
  8.1 0.7 %copy-start.8 = (f32[128]{0:T(128)S(1)}, f32[128]{0:T(128)}, u32[]{:S(2)}) copy-start(f32[128]{0:T(128)} %param.19) | copy-start | bytes 1540

commit v2 on v1

--- a/solution.py
+++ b/solution.py
@@ -45,9 +45,20 @@
 def kernel(
     ncol,
     nmem,
+    columns_hbm,
+    counts_hbm,
+    blocks_hbm,
+    diag_hbm,
+    logperm_hbm,
+    velocity_hbm,
+    direction_hbm,
+    obs_rows_hbm,
+    obs_weight_hbm,
+    prec_hbm,
+    hess_ref,
+    pred_ref,
     columns_ref,
     counts_ref,
-    blocks_hbm,
     diag_ref,
     logperm_ref,
     velocity_ref,
@@ -55,8 +66,6 @@
     obs_rows_ref,
     obs_weight_ref,
     prec_ref,
-    hess_ref,
-    pred_ref,
     blk,
     merged,
     diag_f,
@@ -75,6 +84,7 @@
     za,
     hb,
     pb,
+    in_sem,
     blk_sem,
     zf_s,
     zf_r,
@@ -98,7 +108,7 @@
     quad = lax.div(row, jnp.int32(nmem))
     mem = lax.rem(row, jnp.int32(nmem))
     nrows, nslots, width = blk.shape[0], blk.shape[1], blk.shape[2]
-    share = direction_ref.shape[0] // ncol
+    share = direction_ref.shape[0]
     nblk = nmem * nrows
 
     def device(q, k, c):
@@ -138,24 +148,42 @@
         pl.semaphore_signal(
             barrier, inc=1, device_id=device(q, k, c), device_id_type=pl.DeviceIdType.MESH
         )
+    sources = (
+        (logperm_hbm, logperm_ref),
+        (velocity_hbm, velocity_ref),
+        (direction_hbm.at[pl.ds(col * share, share)], direction_ref),
+        (diag_hbm, diag_ref),
+        (columns_hbm, columns_ref),
+        (counts_hbm, counts_ref),
+        (obs_rows_hbm, obs_rows_ref),
+        (obs_weight_hbm, obs_weight_ref),
+        (prec_hbm, prec_ref),
+    )
+    inputs = [
+        pltpu.make_async_copy(src, dst, in_sem.at[n]) for n, (src, dst) in enumerate(sources)
+    ]
+    for item in inputs:
+        item.start()
     fetches = [
         pltpu.make_async_copy(blocks_hbm.at[i], blk.at[i], blk_sem.at[i]) for i in range(nrows)
     ]
     for fetch in fetches:
         fetch.start()
 
+    for item in inputs[:4]:
+        item.wait()
     alpha = jnp.exp(logperm_ref[...]) * velocity_ref[...]
     for i in range(nrows):
         high, low = split(diag_ref[i].T)
         diag_f[i, :, :width] = high
         diag_f[i, :, width:] = low
-    mine = direction_ref[pl.ds(col * share, share)]
+    mine = direction_ref[...]
     forcing = stack([-alpha[i : i + 1] * mine[:, i, :] for i in range(nrows)])
     base = diag_apply(diag_f, forcing)
 
     def merge(i):
         fetches[i].wait()
-        count = counts_ref[i, 0]
+        count = counts_ref[0, i]
         target = [
             jnp.where(jnp.int32(k) < count, columns_ref[i, k], jnp.int32(-1))
             for k in range(nslots)
@@ -182,6 +210,13 @@
         else:
             pl.when(when)(item.start)
         sent.append((item, when))
+
+    def drain(items):
+        for item, when in items:
+            if when is None:
+                item.wait_send()
+            else:
+                pl.when(when)(item.wait_send)
 
     def spread_along_row(t, piece):
         zf[t, quad] = piece.astype(BF16)
@@ -275,6 +310,8 @@
             pl.semaphore_wait(barrier, len(peers))
         spread_along_row(t, state)
         if t == 0:
+            for item in inputs[4:]:
+                item.wait()
             for i in range(nrows // 2):
                 merge(i)
         forward_to_column(t)
@@ -368,17 +405,14 @@
     gather_wait(pb, (), pb_r)
     for c in range(ncol):
         pred_ref[c * share : (c + 1) * share, :] = pb[c]
+    drain(sent[: 1 - ncol])
     gather_wait(hb, (), hb_r)
     for c in range(ncol):
         piece = hb[c].astype(F32)
         for i in range(nrows):
             hess_ref[c * share : (c + 1) * share, i, :] = block_row(piece, i)
 
-    for item, when in sent:
-        if when is None:
-            item.wait_send()
-        else:
-            pl.when(when)(item.wait_send)
+    drain(sent[1 - ncol :])
 
 
 def per_device(
@@ -401,7 +435,6 @@
     rows = nrows * share
     dma = pltpu.SemaphoreType.DMA
     vmem = pl.BlockSpec(memory_space=pltpu.VMEM)
-    smem = pl.BlockSpec(memory_space=pltpu.SMEM)
 
     def pieces(*lead):
         return pltpu.VMEM(lead + (rows, width), BF16)
@@ -413,9 +446,18 @@
             jax.ShapeDtypeStruct(direction.shape, F32),
             jax.ShapeDtypeStruct((directions, points), F32),
         ),
-        in_specs=[smem, smem, pl.BlockSpec(memory_space=pl.ANY)] + [vmem] * 7,
+        in_specs=[pl.BlockSpec(memory_space=pl.ANY)] * 10,
         out_specs=(vmem, vmem),
         scratch_shapes=[
+            pltpu.SMEM(columns.shape, jnp.int32),
+            pltpu.SMEM((1, nrows), jnp.int32),
+            pltpu.VMEM(inverse_diag.shape, F32),
+            pltpu.VMEM(base_velocity.shape, F32),
+            pltpu.VMEM(base_velocity.shape, F32),
+            pltpu.VMEM((share,) + direction.shape[1:], F32),
+            pltpu.VMEM((1, points), jnp.int32),
+            pltpu.VMEM(obs_weight.shape, F32),
+            pltpu.VMEM((1, points), F32),
             pltpu.VMEM(blocks.shape, BF16),
             pltpu.VMEM((nrows * width, nmem * nrows * width), BF16),
             pltpu.VMEM((nrows, width, 2 * width), BF16),
@@ -434,6 +476,7 @@
             pieces(s, c),
             pieces(c),
             pltpu.VMEM((c, share, points), F32),
+            dma((9,)),
             dma((nrows,)),
             dma((s, c)),
             dma((s, c)),
@@ -453,11 +496,11 @@
             dma((c,)),
         ],
         compiler_params=pltpu.CompilerParams(
-            collective_id=0, has_side_effects=True, vmem_limit_bytes=32 * 1024 * 1024
+            collective_id=0, has_side_effects=True, vmem_limit_bytes=60 * 1024 * 1024
         ),
     )(
         columns,
-        counts,
+        counts.reshape(1, nrows),
         blocks,
         inverse_diag,
         log_inverse_permeability,

time: 62.3 us -> 55.6 us (0.89)
  local copies, waits for them, and re-layouts: 9.37 us -> 2.8 us
    unnamed x21 -> x2, local copies, waits for them, and re-layouts: 9.37 us -> 2.8 us
where the time goes in v2:
time: 55.6 us; the launch traced here: 55.4 us
  Pallas kernels  51.9 us (93%)
  local copies, waits for them, and re-layouts  2.8 us (5%)
  between operations  0.64 us (1%)
    pallas_call x1, Pallas kernels, per_device(): pl.pallas_call(functools.partial(kernel, ncol, nmem), out_shape=(jax.Shap...  51.9 us
    unnamed x2, local copies, waits for them, and re-layouts  2.8 us

profile of v2, /device:TPU:0, one launch (start us, length us, event | category | flops | bytes accessed | tf_op | source)
XLA Modules:
  0.0 55.4 jit_solution(14601868700587110742)
XLA Ops:
  0.6 51.9 %shard_map.113 = (f32[32,4,128]{2,1,0:T(4,128)}, f32[32,128]{1,0:T(8,128)}) custom-call(s32[4,12]{1,0:T(4,128)} %columns_hbm.1, s32[1,4]{1,0:T(1,128)} %bitcast.3, bf16[4,12,128,128]{3,2,1,0:T(8,128)(2,1)} %blocks_hbm.1, f32[4,128,128]{2,1,0:T(8,128)} %diag_hbm.1, f32[4,128]{1,0:T(4,128)} %logperm_hbm.1, f32[4,128]{1,0:T(4,128)} %velocity_hbm.1, ...), custom_call_target="tpu_custom_call" | custom-call | tf_op jit(solution)/shard_map/pallas_call | solution.py:443
  52.6 1.5 %copy.14 = f32[32,4,128]{2,1,0:T(4,128)} copy(f32[32,4,128]{2,1,0:T(4,128)} %get-tuple-element.4) | data formatting | bytes 131072
  54.1 1.3 %copy.15 = f32[32,128]{1,0:T(8,128)} copy(f32[32,128]{1,0:T(8,128)} %get-tuple-element.5) | data formatting | bytes 32768

commit v3 on v2

--- a/solution.py
+++ b/solution.py
@@ -80,8 +80,6 @@
     yb,
     ad_out,
     ad_in,
-    za_out,
-    za,
     hb,
     pb,
     in_sem,
@@ -96,8 +94,6 @@
     yb_r,
     ad_s,
     ad_r,
-    za_s,
-    za_r,
     hb_s,
     hb_r,
     pb_s,
@@ -137,17 +133,31 @@
         return stack([wide_matmul(block_row(piece, i), pairs[i]) for i in range(nrows)])
 
     barrier = pltpu.get_barrier_semaphore()
-    peers = [(flip(quad, f, ncol), mem, col) for f in range(1, ncol)]
+    peers = [((quad, mem, flip(col, e, ncol)), None) for e in range(1, ncol)]
+    peers += [((flip(quad, f, ncol), mem, col), None) for f in range(1, ncol)]
     peers += [
-        (quad, flip(mem, x, nmem), flip(col, e, ncol))
+        ((quad, flip(mem, x, nmem), flip(col, e, ncol)), None)
         for e in range(ncol)
-        for x in range(nmem)
-        if e or x
+        for x in range(1, nmem)
     ]
-    for q, k, c in peers:
+    off = quad != col
+    for f in range(ncol):
+        for x in range(nmem):
+            when = None if f or x else off
+            peers.append(((flip(quad, f, ncol), flip(mem, x, nmem), quad), when))
+            peers.append(((col, flip(mem, x, nmem), flip(col, f, ncol)), when))
+
+    def greet(target):
         pl.semaphore_signal(
-            barrier, inc=1, device_id=device(q, k, c), device_id_type=pl.DeviceIdType.MESH
+            barrier, inc=1, device_id=device(*target), device_id_type=pl.DeviceIdType.MESH
         )
+
+    for target, when in peers:
+        if when is None:
+            greet(target)
+        else:
+            pl.when(when)(functools.partial(greet, target))
+    greeted = sum(1 if when is None else when.astype(jnp.int32) for _, when in peers)
     sources = (
         (logperm_hbm, logperm_ref),
         (velocity_hbm, velocity_ref),
@@ -307,7 +317,7 @@
     state = base
     for t in range(SWEEPS):
         if t == 0:
-            pl.semaphore_wait(barrier, len(peers))
+            pl.semaphore_wait(barrier, greeted)
         spread_along_row(t, state)
         if t == 0:
             for item in inputs[4:]:
@@ -359,43 +369,34 @@
                         for i in range(nrows)
                     ]
                 ).astype(BF16)
-        for e in range(ncol):
+        for e in reversed(range(ncol)):
             for x in range(nmem):
-                if e or x:
-                    k, c = flip(mem, x, nmem), flip(col, e, ncol)
-                    start(
-                        copy(
-                            ad_out.at[t, k, c],
-                            ad_in.at[t, mem, col],
-                            ad_s.at[t, x, e],
-                            ad_r.at[t, mem, col],
-                            device(quad, k, c),
-                        )
-                    )
-        ad_in[t, mem, col] = ad_out[t, mem, col]
-        for e in range(ncol):
-            c = flip(col, e, ncol)
+                k, c = flip(mem, x, nmem), flip(col, e, ncol)
+                start(
+                    copy(
+                        ad_out.at[t, k, c],
+                        ad_in.at[t, mem, quad],
+                        ad_s.at[t, x, e],
+                        ad_r.at[t, mem, quad],
+                        device(col, k, c),
+                    ),
+                    None if e or x else off,
+                )
+
+        @pl.when(quad == col)
+        def _():
+            ad_in[t, mem, quad] = ad_out[t, mem, col]
+
+        total = 0.0
+        for f in range(ncol):
             for x in range(nmem):
-                if e or x:
-                    k = flip(mem, x, nmem)
-                    landed(ad_in.at[t, k, c], ad_r.at[t, k, c])
-            total = sum(ad_in[t, k, c].astype(F32) for k in range(nmem))
-            za_out[t, c] = total.astype(BF16)
-            start(
-                copy(
-                    za_out.at[t, c],
-                    za.at[t, quad],
-                    za_s.at[t, e],
-                    za_r.at[t, quad],
-                    device(c, mem, col),
-                ),
-                c != quad,
-            )
-        total = za_out[t, quad].astype(F32)
-        for f in range(1, ncol):
-            q = flip(quad, f, ncol)
-            landed(za.at[t, q], za_r.at[t, q])
-            total = total + za[t, q].astype(F32)
+                k, q = flip(mem, x, nmem), flip(quad, f, ncol)
+                wait = functools.partial(landed, ad_in.at[t, k, q], ad_r.at[t, k, q])
+                if f or x:
+                    wait()
+                else:
+                    pl.when(off)(wait)
+                total = total + ad_in[t, k, q].astype(F32)
         adjoint = diag_apply(diag_a, force - total)
 
     hb[col] = stack(
@@ -413,6 +414,17 @@
             hess_ref[c * share : (c + 1) * share, i, :] = block_row(piece, i)
 
     drain(sent[1 - ncol :])
+
+
+def hand_over(hess_from, pred_from, hess_to, pred_to, sem):
+    moves = [
+        pltpu.make_async_copy(hess_from, hess_to, sem.at[0]),
+        pltpu.make_async_copy(pred_from, pred_to, sem.at[1]),
+    ]
+    for move in moves:
+        move.start()
+    for move in moves:
+        move.wait()
 
 
 def per_device(
@@ -440,7 +452,7 @@
         return pltpu.VMEM(lead + (rows, width), BF16)
 
     s, c, g = SWEEPS, ncol, nmem
-    return pl.pallas_call(
+    results = pl.pallas_call(
         functools.partial(kernel, ncol, nmem),
         out_shape=(
             jax.ShapeDtypeStruct(direction.shape, F32),
@@ -472,8 +484,6 @@
             pieces(s, c),
             pieces(s, g, c),
             pieces(s, g, c),
-            pieces(s, c),
-            pieces(s, c),
             pieces(c),
             pltpu.VMEM((c, share, points), F32),
             dma((9,)),
@@ -488,8 +498,6 @@
             dma((s, c)),
             dma((s, g, c)),
             dma((s, g, c)),
-            dma((s, c)),
-            dma((s, c)),
             dma((c,)),
             dma((c,)),
             dma((c,)),
@@ -510,6 +518,15 @@
         obs_weight,
         noise_prec.reshape(1, points),
     )
+    anywhere = pl.BlockSpec(memory_space=pl.ANY)
+    return pl.pallas_call(
+        hand_over,
+        out_shape=tuple(jax.ShapeDtypeStruct(x.shape, x.dtype) for x in results),
+        in_specs=[anywhere] * 2,
+        out_specs=(anywhere, anywhere),
+        scratch_shapes=[dma((2,))],
+        compiler_params=pltpu.CompilerParams(vmem_limit_bytes=60 * 1024 * 1024),
+    )(*results)
 
 
 def solution(mesh):

time: 55.6 us -> 52.5 us (0.944)
  local copies, waits for them, and re-layouts: 2.8 us -> 0 us
    pallas_call x1, Pallas kernels: 51.9 us -> 48.1 us  [per_device(): pl.pallas_call(functools.partial(kernel, ncol, nmem), out_shape=(jax.Shap...]
    pallas_call x0 -> x1, Pallas kernels: none -> 3.6 us  [per_device(): pl.pallas_call(hand_over, out_shape=tuple((jax.ShapeDtypeStruct(x.shape,...]
    unnamed x2 -> x0, local copies, waits for them, and re-layouts: 2.8 us -> none
where the time goes in v3:
time: 52.5 us; the launch traced here: 52.3 us
  Pallas kernels  51.7 us (98%)
  between operations  0.64 us (1%)
    pallas_call x1, Pallas kernels, per_device(): pl.pallas_call(functools.partial(kernel, ncol, nmem), out_shape=(jax.Shap...  48.1 us
    pallas_call x1, Pallas kernels, per_device(): pl.pallas_call(hand_over, out_shape=tuple((jax.ShapeDtypeStruct(x.shape,...  3.6 us

profile of v3, /device:TPU:0, one launch (start us, length us, event | category | flops | bytes accessed | tf_op | source)
XLA Modules:
  0.0 52.3 jit_solution(492165545063868598)
XLA Ops:
  0.6 48.1 %shard_map.113 = (f32[32,4,128]{2,1,0:T(4,128)}, f32[32,128]{1,0:T(8,128)}) custom-call(s32[4,12]{1,0:T(4,128)} %columns_hbm.1, s32[1,4]{1,0:T(1,128)} %bitcast.3, bf16[4,12,128,128]{3,2,1,0:T(8,128)(2,1)} %blocks_hbm.1, f32[4,128,128]{2,1,0:T(8,128)} %diag_hbm.1, f32[4,128]{1,0:T(4,128)} %logperm_hbm.1, f32[4,128]{1,0:T(4,128)} %velocity_hbm.1, ...), custom_call_target="tpu_custom_call" | custom-call | tf_op jit(solution)/shard_map/pallas_call | solution.py:455
  48.7 3.6 %shard_map.114 = (f32[32,4,128]{2,1,0:T(4,128)}, f32[32,128]{1,0:T(8,128)}) custom-call(f32[32,4,128]{2,1,0:T(4,128)} %get-tuple-element.4.hess_from, f32[32,128]{1,0:T(8,128)} %get-tuple-element.5.pred_from), custom_call_target="tpu_custom_call" | custom-call | tf_op jit(solution)/shard_map/pallas_call | solution.py:522

commit v4 on v3

--- a/solution.py
+++ b/solution.py
@@ -84,8 +84,6 @@
     pb,
     in_sem,
     blk_sem,
-    zf_s,
-    zf_r,
     xf_s,
     xf_r,
     rs_s,
@@ -134,12 +132,6 @@
 
     barrier = pltpu.get_barrier_semaphore()
     peers = [((quad, mem, flip(col, e, ncol)), None) for e in range(1, ncol)]
-    peers += [((flip(quad, f, ncol), mem, col), None) for f in range(1, ncol)]
-    peers += [
-        ((quad, flip(mem, x, nmem), flip(col, e, ncol)), None)
-        for e in range(ncol)
-        for x in range(1, nmem)
-    ]
     off = quad != col
     for f in range(ncol):
         for x in range(nmem):
@@ -228,44 +220,34 @@
             else:
                 pl.when(when)(item.wait_send)
 
-    def spread_along_row(t, piece):
-        zf[t, quad] = piece.astype(BF16)
-        for f in range(1, ncol):
-            q = flip(quad, f, ncol)
-            start(
-                copy(
-                    zf.at[t, quad],
-                    zf.at[t, quad],
-                    zf_s.at[t, f],
-                    zf_r.at[t, quad],
-                    device(q, mem, col),
-                )
-            )
-
-    def forward_to_column(t):
-        for f in range(ncol):
-            q = flip(quad, f, ncol)
-            if f:
-                landed(zf.at[t, q], zf_r.at[t, q])
+    def spread(t, piece):
+        zf[t] = piece.astype(BF16)
+        for f in reversed(range(ncol)):
             for x in range(nmem):
                 start(
                     copy(
-                        zf.at[t, q],
+                        zf.at[t],
                         xf.at[t, mem, col],
                         xf_s.at[t, f, x],
                         xf_r.at[t, mem, col],
-                        device(quad, flip(mem, x, nmem), q),
+                        device(flip(quad, f, ncol), flip(mem, x, nmem), quad),
                     ),
-                    None if x else q != col,
+                    None if f or x else off,
                 )
-        xf[t, mem, col] = zf[t, col]
+
+        @pl.when(quad == col)
+        def _():
+            xf[t, mem, col] = zf[t]
 
     def column_state(t):
         for e in range(ncol):
             for x in range(nmem):
+                k, c = flip(mem, x, nmem), flip(col, e, ncol)
+                wait = functools.partial(landed, xf.at[t, k, c], xf_r.at[t, k, c])
                 if e or x:
-                    k, c = flip(mem, x, nmem), flip(col, e, ncol)
-                    landed(xf.at[t, k, c], xf_r.at[t, k, c])
+                    wait()
+                else:
+                    pl.when(off)(wait)
         lanes = []
         for k in range(nmem):
             pieces = [xf[t, k, c].astype(F32) for c in range(ncol)]
@@ -318,15 +300,11 @@
     for t in range(SWEEPS):
         if t == 0:
             pl.semaphore_wait(barrier, greeted)
-        spread_along_row(t, state)
+        spread(t, state)
         if t == 0:
             for item in inputs[4:]:
                 item.wait()
-            for i in range(nrows // 2):
-                merge(i)
-        forward_to_column(t)
-        if t == 0:
-            for i in range(nrows // 2, nrows):
+            for i in range(nrows):
                 merge(i)
         terms = matmul_t(column_state(t), merged[...])
         if t == 0:
@@ -477,7 +455,7 @@
             pltpu.VMEM((width, 2 * points), BF16),
             pltpu.VMEM((points, 2 * width), BF16),
             pltpu.VMEM((s, c, rows, width), F32),
-            pieces(s, c),
+            pieces(s),
             pieces(s, g, c),
             pieces(s, c),
             pieces(s, c),
@@ -488,8 +466,6 @@
             pltpu.VMEM((c, share, points), F32),
             dma((9,)),
             dma((nrows,)),
-            dma((s, c)),
-            dma((s, c)),
             dma((s, c, g)),
             dma((s, g, c)),
             dma((s, c)),

time: 52.5 us -> 47.8 us (0.910)
  Pallas kernels: 51.7 us -> 47 us
    pallas_call x1, Pallas kernels: 48.1 us -> 43.4 us  [per_device(): pl.pallas_call(functools.partial(kernel, ncol, nmem), out_shape=(jax.Shap...]
where the time goes in v4:
time: 47.8 us; the launch traced here: 47.7 us
  Pallas kernels  47 us (98%)
  between operations  0.64 us (1%)
    pallas_call x1, Pallas kernels, per_device(): pl.pallas_call(functools.partial(kernel, ncol, nmem), out_shape=(jax.Shap...  43.4 us
    pallas_call x1, Pallas kernels, per_device(): pl.pallas_call(hand_over, out_shape=tuple((jax.ShapeDtypeStruct(x.shape,...  3.6 us

profile of v4, /device:TPU:0, one launch (start us, length us, event | category | flops | bytes accessed | tf_op | source)
XLA Modules:
  0.0 47.7 jit_solution(6962114635387318817)
XLA Ops:
  0.6 43.4 %shard_map.113 = (f32[32,4,128]{2,1,0:T(4,128)}, f32[32,128]{1,0:T(8,128)}) custom-call(s32[4,12]{1,0:T(4,128)} %columns_hbm.1, s32[1,4]{1,0:T(1,128)} %bitcast.3, bf16[4,12,128,128]{3,2,1,0:T(8,128)(2,1)} %blocks_hbm.1, f32[4,128,128]{2,1,0:T(8,128)} %diag_hbm.1, f32[4,128]{1,0:T(4,128)} %logperm_hbm.1, f32[4,128]{1,0:T(4,128)} %velocity_hbm.1, ...), custom_call_target="tpu_custom_call" | custom-call | tf_op jit(solution)/shard_map/pallas_call | solution.py:433
  44.1 3.6 %shard_map.114 = (f32[32,4,128]{2,1,0:T(4,128)}, f32[32,128]{1,0:T(8,128)}) custom-call(f32[32,4,128]{2,1,0:T(4,128)} %get-tuple-element.4.hess_from, f32[32,128]{1,0:T(8,128)} %get-tuple-element.5.pred_from), custom_call_target="tpu_custom_call" | custom-call | tf_op jit(solution)/shard_map/pallas_call | solution.py:498

commit v5 on v4

--- a/solution.py
+++ b/solution.py
@@ -81,7 +81,8 @@
     ad_out,
     ad_in,
     hb,
-    pb,
+    whole,
+    base_all,
     in_sem,
     blk_sem,
     xf_s,
@@ -94,16 +95,17 @@
     ad_r,
     hb_s,
     hb_r,
-    pb_s,
-    pb_r,
+    whole_s,
+    whole_r,
 ):
     row = lax.axis_index("row")
     col = lax.axis_index("col")
     quad = lax.div(row, jnp.int32(nmem))
     mem = lax.rem(row, jnp.int32(nmem))
     nrows, nslots, width = blk.shape[0], blk.shape[1], blk.shape[2]
-    share = direction_ref.shape[0]
+    share = direction_ref.shape[0] // ncol
     nblk = nmem * nrows
+    ndir = share * ncol
 
     def device(q, k, c):
         return (q * nmem + k, c)
@@ -153,7 +155,7 @@
     sources = (
         (logperm_hbm, logperm_ref),
         (velocity_hbm, velocity_ref),
-        (direction_hbm.at[pl.ds(col * share, share)], direction_ref),
+        (direction_hbm, direction_ref),
         (diag_hbm, diag_ref),
         (columns_hbm, columns_ref),
         (counts_hbm, counts_ref),
@@ -179,7 +181,7 @@
         high, low = split(diag_ref[i].T)
         diag_f[i, :, :width] = high
         diag_f[i, :, width:] = low
-    mine = direction_ref[...]
+    mine = direction_ref[pl.ds(col * share, share)]
     forcing = stack([-alpha[i : i + 1] * mine[:, i, :] for i in range(nrows)])
     base = diag_apply(diag_f, forcing)
 
@@ -203,6 +205,10 @@
             return carry
 
         lax.fori_loop(0, nblk // 2, body, 0)
+        high, low = split(diag_ref[i])
+        own = slice(i * width, (i + 1) * width)
+        both = matmul(jnp.concatenate([high, low], axis=0), merged[own, :])
+        merged[own, :] = (both[:width] + both[width:]).astype(BF16)
 
     sent = []
 
@@ -255,11 +261,11 @@
                 lanes.append(stack([block_row(piece, i) for piece in pieces]))
         return jnp.concatenate(lanes, axis=1).astype(BF16)
 
-    def sum_over_columns(t, terms):
+    def sum_start(t, terms):
         for c in range(ncol):
             rows = terms[c * share : (c + 1) * share]
             piece = stack([rows[:, i * width : (i + 1) * width] for i in range(nrows)])
-            part[t, c] = piece
+            part[c] = piece
             rs_out[t, c] = piece.astype(BF16)
         for e in range(1, ncol):
             c = flip(col, e, ncol)
@@ -272,12 +278,23 @@
                     device(quad, mem, c),
                 )
             )
-        total = part[t, col]
+
+    def sum_finish(t):
+        total = part[col]
         for e in range(1, ncol):
             c = flip(col, e, ncol)
             landed(rs_in.at[t, c], rs_r.at[t, c])
             total = total + rs_in[t, c].astype(F32)
         return total
+
+    def by_block_row(values):
+        return stack([values[:, i * width : (i + 1) * width] for i in range(nrows)])
+
+    def by_lane(values):
+        count = values.shape[0] // nrows
+        return jnp.concatenate(
+            [values[i * count : (i + 1) * count] for i in range(nrows)], axis=1
+        )
 
     def gather_start(buf, at, send, recv):
         for e in range(1, ncol):
@@ -296,48 +313,69 @@
             c = flip(col, e, ncol)
             landed(buf.at[at + (c,)], recv.at[at + (c,)])
 
-    state = base
-    for t in range(SWEEPS):
+    pl.semaphore_wait(barrier, greeted)
+    spread(0, base)
+    for item in inputs[4:]:
+        item.wait()
+    for i in range(nrows):
+        merge(i)
+    for t in range(SWEEPS - 1):
+        sum_start(t, matmul_t(column_state(t), merged[...]))
         if t == 0:
-            pl.semaphore_wait(barrier, greeted)
-        spread(t, state)
-        if t == 0:
-            for item in inputs[4:]:
-                item.wait()
-            for i in range(nrows):
-                merge(i)
-        terms = matmul_t(column_state(t), merged[...])
-        if t == 0:
-            for i in range(nrows):
-                high, low = split(diag_ref[i])
-                diag_a[i, :, :width] = high
-                diag_a[i, :, width:] = low
-            high, low = split(obs_weight_ref[...])
+            every = stack([-alpha[i : i + 1] * direction_ref[:, i, :] for i in range(nrows)])
+            base_all[...] = by_lane(
+                stack(
+                    [
+                        wide_matmul(every[i * ndir : (i + 1) * ndir], diag_f[i])
+                        for i in range(nrows)
+                    ]
+                )
+            )
             points = obs_weight_ref.shape[0]
-            obs_a[:, :width] = high
-            obs_a[:, width:] = low
             high, low = split(obs_weight_ref[...].T)
             obs_f[:, :points] = high
             obs_f[:, points:] = low
-        state = base - diag_apply(diag_f, sum_over_columns(t, terms))
-
-    sampled = wide_matmul(state, obs_f[...])
+        spread(t + 1, base - sum_finish(t))
+
+    terms = matmul_t(column_state(SWEEPS - 1), merged[...])
+    whole[col] = terms.astype(BF16)
+    for e in range(1, ncol):
+        start(
+            copy(
+                whole.at[col],
+                whole.at[col],
+                whole_s.at[e],
+                whole_r.at[col],
+                device(quad, mem, flip(col, e, ncol)),
+            )
+        )
+    high, low = split(obs_weight_ref[...])
+    obs_a[:, :width] = high
+    obs_a[:, width:] = low
+    for e in range(1, ncol):
+        c = flip(col, e, ncol)
+        landed(whole.at[c], whole_r.at[c])
+    state = base_all[...] - sum(whole[c].astype(F32) for c in range(ncol))
+
+    sampled = wide_matmul(by_block_row(state), obs_f[...])
     chosen = [(obs_rows_ref[...] == i).astype(F32) for i in range(nrows)]
-    predicted = sum(block_row(sampled, i) * chosen[i] for i in range(nrows))
+    predicted = sum(sampled[i * ndir : (i + 1) * ndir] * chosen[i] for i in range(nrows))
     weighted = predicted * prec_ref[...]
-    force = -wide_matmul(stack([weighted * chosen[i] for i in range(nrows)]), obs_a[...])
-    adjoint = diag_apply(diag_a, force)
+    force_all = by_lane(
+        -wide_matmul(stack([weighted * chosen[i] for i in range(nrows)]), obs_a[...])
+    )
+    operand = force_all.astype(BF16)
 
     for t in range(SWEEPS):
-        yb[t, col] = adjoint.astype(BF16)
-        gather_start(yb, (t,), yb_s, yb_r)
-        if t == 0:
-            pb[col] = predicted
-            gather_start(pb, (), pb_s, pb_r)
-        gather_wait(yb, (t,), yb_r)
-        pieces = [yb[t, c].astype(F32) for c in range(ncol)]
-        lanes = [stack([block_row(piece, i) for piece in pieces]) for i in range(nrows)]
-        terms = matmul(jnp.concatenate(lanes, axis=1).astype(BF16), merged[...])
+        if t:
+            yb[t, col] = adjoint.astype(BF16)
+            gather_start(yb, (t,), yb_s, yb_r)
+            gather_wait(yb, (t,), yb_r)
+            pieces = [yb[t, c].astype(F32) for c in range(ncol)]
+            operand = jnp.concatenate(
+                [stack([block_row(piece, i) for piece in pieces]) for i in range(nrows)], axis=1
+            ).astype(BF16)
+        terms = matmul(operand, merged[...])
         for k in range(nmem):
             for c in range(ncol):
                 rows = terms[c * share : (c + 1) * share]
@@ -365,6 +403,15 @@
         def _():
             ad_in[t, mem, quad] = ad_out[t, mem, col]
 
+        if t == 0:
+            pred_ref[...] = predicted
+            for c in range(ncol):
+                part[c] = by_block_row(force_all[c * share : (c + 1) * share])
+            force = part[col]
+            for i in range(nrows):
+                high, low = split(diag_ref[i])
+                diag_a[i, :, :width] = high
+                diag_a[i, :, width:] = low
         total = 0.0
         for f in range(ncol):
             for x in range(nmem):
@@ -375,15 +422,13 @@
                 else:
                     pl.when(off)(wait)
                 total = total + ad_in[t, k, q].astype(F32)
-        adjoint = diag_apply(diag_a, force - total)
-
+        adjoint = force - total
+
+    adjoint = diag_apply(diag_a, adjoint)
     hb[col] = stack(
         [-alpha[i : i + 1] * block_row(adjoint, i) for i in range(nrows)]
     ).astype(BF16)
     gather_start(hb, (), hb_s, hb_r)
-    gather_wait(pb, (), pb_r)
-    for c in range(ncol):
-        pred_ref[c * share : (c + 1) * share, :] = pb[c]
     drain(sent[: 1 - ncol])
     gather_wait(hb, (), hb_r)
     for c in range(ncol):
@@ -392,17 +437,6 @@
             hess_ref[c * share : (c + 1) * share, i, :] = block_row(piece, i)
 
     drain(sent[1 - ncol :])
-
-
-def hand_over(hess_from, pred_from, hess_to, pred_to, sem):
-    moves = [
-        pltpu.make_async_copy(hess_from, hess_to, sem.at[0]),
-        pltpu.make_async_copy(pred_from, pred_to, sem.at[1]),
-    ]
-    for move in moves:
-        move.start()
-    for move in moves:
-        move.wait()
 
 
 def per_device(
@@ -430,7 +464,7 @@
         return pltpu.VMEM(lead + (rows, width), BF16)
 
     s, c, g = SWEEPS, ncol, nmem
-    results = pl.pallas_call(
+    return pl.pallas_call(
         functools.partial(kernel, ncol, nmem),
         out_shape=(
             jax.ShapeDtypeStruct(direction.shape, F32),
@@ -444,7 +478,7 @@
             pltpu.VMEM(inverse_diag.shape, F32),
             pltpu.VMEM(base_velocity.shape, F32),
             pltpu.VMEM(base_velocity.shape, F32),
-            pltpu.VMEM((share,) + direction.shape[1:], F32),
+            pltpu.VMEM(direction.shape, F32),
             pltpu.VMEM((1, points), jnp.int32),
             pltpu.VMEM(obs_weight.shape, F32),
             pltpu.VMEM((1, points), F32),
@@ -454,7 +488,7 @@
             pltpu.VMEM((nrows, width, 2 * width), BF16),
             pltpu.VMEM((width, 2 * points), BF16),
             pltpu.VMEM((points, 2 * width), BF16),
-            pltpu.VMEM((s, c, rows, width), F32),
+            pltpu.VMEM((c, rows, width), F32),
             pieces(s),
             pieces(s, g, c),
             pieces(s, c),
@@ -463,7 +497,8 @@
             pieces(s, g, c),
             pieces(s, g, c),
             pieces(c),
-            pltpu.VMEM((c, share, points), F32),
+            pltpu.VMEM((c, directions, nrows * width), BF16),
+            pltpu.VMEM((directions, nrows * width), F32),
             dma((9,)),
             dma((nrows,)),
             dma((s, c, g)),
@@ -494,15 +529,6 @@
         obs_weight,
         noise_prec.reshape(1, points),
     )
-    anywhere = pl.BlockSpec(memory_space=pl.ANY)
-    return pl.pallas_call(
-        hand_over,
-        out_shape=tuple(jax.ShapeDtypeStruct(x.shape, x.dtype) for x in results),
-        in_specs=[anywhere] * 2,
-        out_specs=(anywhere, anywhere),
-        scratch_shapes=[dma((2,))],
-        compiler_params=pltpu.CompilerParams(vmem_limit_bytes=60 * 1024 * 1024),
-    )(*results)
 
 
 def solution(mesh):

time: 47.8 us -> 44.6 us (0.933)
  Pallas kernels: 47 us -> 40.9 us
  local copies, waits for them, and re-layouts: 0 us -> 2.8 us
    pallas_call x1 -> x0, Pallas kernels: 3.6 us -> none  [per_device(): pl.pallas_call(hand_over, out_shape=tuple((jax.ShapeDtypeStruct(x.shape,...]
    unnamed x0 -> x2, local copies, waits for them, and re-layouts: none -> 2.8 us
    pallas_call x1, Pallas kernels: 43.4 us -> 40.9 us  [per_device(): pl.pallas_call(functools.partial(kernel, ncol, nmem), out_shape=(jax.Shap...]
where the time goes in v5:
time: 44.6 us; the launch traced here: 44.3 us
  Pallas kernels  40.9 us (92%)
  local copies, waits for them, and re-layouts  2.8 us (6%)
  between operations  0.64 us (1%)
    pallas_call x1, Pallas kernels, per_device(): pl.pallas_call(functools.partial(kernel, ncol, nmem), out_shape=(jax.Shap...  40.9 us
    unnamed x2, local copies, waits for them, and re-layouts  2.8 us

profile of v5, /device:TPU:0, one launch (start us, length us, event | category | flops | bytes accessed | tf_op | source)
XLA Modules:
  0.0 44.3 jit_solution(6674688027002966833)
XLA Ops:
  0.6 40.9 %shard_map.113 = (f32[32,4,128]{2,1,0:T(4,128)}, f32[32,128]{1,0:T(8,128)}) custom-call(s32[4,12]{1,0:T(4,128)} %columns_hbm.1, s32[1,4]{1,0:T(1,128)} %bitcast.3, bf16[4,12,128,128]{3,2,1,0:T(8,128)(2,1)} %blocks_hbm.1, f32[4,128,128]{2,1,0:T(8,128)} %diag_hbm.1, f32[4,128]{1,0:T(4,128)} %logperm_hbm.1, f32[4,128]{1,0:T(4,128)} %velocity_hbm.1, ...), custom_call_target="tpu_custom_call" | custom-call | tf_op jit(solution)/shard_map/pallas_call | solution.py:467
  41.5 1.5 %copy.14 = f32[32,4,128]{2,1,0:T(4,128)} copy(f32[32,4,128]{2,1,0:T(4,128)} %get-tuple-element.4) | data formatting | bytes 131072
  43.0 1.3 %copy.15 = f32[32,128]{1,0:T(8,128)} copy(f32[32,128]{1,0:T(8,128)} %get-tuple-element.5) | data formatting | bytes 32768

commit v6 on v5

--- a/solution.py
+++ b/solution.py
@@ -105,6 +105,7 @@
     nrows, nslots, width = blk.shape[0], blk.shape[1], blk.shape[2]
     share = direction_ref.shape[0] // ncol
     nblk = nmem * nrows
+    chunk = 32
     ndir = share * ncol
 
     def device(q, k, c):
@@ -193,18 +194,20 @@
             for k in range(nslots)
         ]
 
-        def body(pair, carry):
-            for half in range(2):
-                j = pair * 2 + half
-                total = jnp.zeros((width, width), F32)
-                for k in range(nslots):
+        def body(step, carry):
+            rows = pl.ds(pl.multiple_of(step * chunk, chunk), chunk)
+            totals = [jnp.zeros((chunk, width), F32) for _ in range(nblk)]
+            for k in range(nslots):
+                values = blk[i, k, rows, :].astype(F32)
+                for j in range(nblk):
                     keep = jnp.where(target[k] == j, jnp.float32(1), jnp.float32(0))
-                    total = total + keep * blk[i, k].astype(F32)
-                at = pl.ds(pl.multiple_of(j * width, width), width)
-                merged[i * width : (i + 1) * width, at] = total.astype(BF16)
+                    totals[j] = totals[j] + keep * values
+            at = pl.ds(pl.multiple_of(i * width + step * chunk, chunk), chunk)
+            for j in range(nblk):
+                merged[at, j * width : (j + 1) * width] = totals[j].astype(BF16)
             return carry
 
-        lax.fori_loop(0, nblk // 2, body, 0)
+        lax.fori_loop(0, width // chunk, body, 0)
         high, low = split(diag_ref[i])
         own = slice(i * width, (i + 1) * width)
         both = matmul(jnp.concatenate([high, low], axis=0), merged[own, :])

time: 44.6 us -> 44.6 us (level)
  no operation moved by 1% of the time
where the time goes in v6:
time: 44.6 us; the launch traced here: 44.3 us
  Pallas kernels  40.9 us (92%)
  local copies, waits for them, and re-layouts  2.8 us (6%)
  between operations  0.64 us (1%)
    pallas_call x1, Pallas kernels, per_device(): pl.pallas_call(functools.partial(kernel, ncol, nmem), out_shape=(jax.Shap...  40.9 us
    unnamed x2, local copies, waits for them, and re-layouts  2.8 us

profile of v6, /device:TPU:0, one launch (start us, length us, event | category | flops | bytes accessed | tf_op | source)
XLA Modules:
  0.0 44.3 jit_solution(16715475439640528156)
XLA Ops:
  0.6 40.9 %shard_map.113 = (f32[32,4,128]{2,1,0:T(4,128)}, f32[32,128]{1,0:T(8,128)}) custom-call(s32[4,12]{1,0:T(4,128)} %columns_hbm.1, s32[1,4]{1,0:T(1,128)} %bitcast.3, bf16[4,12,128,128]{3,2,1,0:T(8,128)(2,1)} %blocks_hbm.1, f32[4,128,128]{2,1,0:T(8,128)} %diag_hbm.1, f32[4,128]{1,0:T(4,128)} %logperm_hbm.1, f32[4,128]{1,0:T(4,128)} %velocity_hbm.1, ...), custom_call_target="tpu_custom_call" | custom-call | tf_op jit(solution)/shard_map/pallas_call | solution.py:470
  41.5 1.5 %copy.14 = f32[32,4,128]{2,1,0:T(4,128)} copy(f32[32,4,128]{2,1,0:T(4,128)} %get-tuple-element.4) | data formatting | bytes 131072
  43.0 1.3 %copy.15 = f32[32,128]{1,0:T(8,128)} copy(f32[32,128]{1,0:T(8,128)} %get-tuple-element.5) | data formatting | bytes 32768
